TPU v7x, 128 devices: a whole 4x4x4 slice. The times are simulated.
128 devices in a mesh: grp: 4 (over y_lo, core), blk: 32 (over z, y_hi, x).
Axes of the slice: x: 4, y: 4 (y_hi: 2, y_lo: 2; y = y_hi * 2 + y_lo), z: 4, core: 2. Of those that a mesh axis runs over, the one named last changes fastest.
Arguments:
- unlabeled: bfloat16 [65536, 1024], P('blk'), may hold values from -10 to 10
- labeled: bfloat16 [131072, 1024], P(('grp', 'blk')), may hold values from -5 to 5
- picks: int32 [128], replicated, may hold values from 0 to 65535, as said below
Outputs:
- nearest: float32 [65536], P('blk')
Inputs may be any that keep to these rules, and one draw needn't show every extreme that they name: `picks`: indices may repeat; row 0 and row 65535 are always among them.
All inputs are finite; a program needn't handle non-finite values.
Results may differ from a plain program's by a relative error of at most 0.0003.
Values may be sent and summed in bfloat16 or wider, within the bound.
A program may use at most 64 MiB of HBM per device.

v0:
```python
import jax
import jax.numpy as jnp
from jax import lax
from jax.sharding import PartitionSpec as P

STEPS = 2


def from_behind(block, axis, distance):
    devices = range(lax.axis_size(axis))
    route = [((i - distance) % len(devices), i) for i in devices]
    return lax.ppermute(block, axis, route)


def squares(rows):
    wide = rows.astype(jnp.float32)
    return jnp.sum(wide * wide, axis=1)


def least(rows, rows_sq, others, width):
    others_sq = squares(others)
    inner = lax.dot_general(
        rows, others, (((1,), (1,)), ((), ())), preferred_element_type=jnp.float32
    )
    scaled = (rows_sq[:, None] + others_sq[None, :] - 2.0 * inner) / width
    return jnp.min(scaled, axis=1)


def body(unlabeled, labeled, picks):
    width = unlabeled.shape[1]
    rows_dev = unlabeled.shape[0]
    rows_sq = squares(unlabeled)
    labeled_min = least(unlabeled, rows_sq, labeled, width)
    moving = labeled
    for step in range(STEPS):
        moving = from_behind(moving, "blk", 1)
        labeled_min = jnp.minimum(labeled_min, least(unlabeled, rows_sq, moving, width))
    offset = lax.axis_index("blk") * rows_dev
    local = picks - offset
    owned = (local >= 0) & (local < rows_dev)
    taken = unlabeled[jnp.clip(local, 0, rows_dev - 1)]
    chosen = jnp.where(owned[:, None], taken.astype(jnp.float32), 0.0)
    pick_rows = lax.psum(chosen.astype(jnp.bfloat16), "blk")
    pick_min = least(unlabeled, rows_sq, pick_rows, width)
    combined = jnp.minimum(labeled_min, pick_min)
    combined = lax.pmin(combined, "grp")
    return combined


def solution(mesh):
    return jax.shard_map(
        body,
        mesh=mesh,
        in_specs=(P("blk", None), P(("grp", "blk"), None), P()),
        out_specs=P("blk"),
        check_vma=False,
    )
```

profile of v0, /device:TPU:1, one launch (start us, length us, event | category | flops | bytes accessed | tf_op | source)
XLA Modules:
  0.0 402.8 jit_solution(1273485559894584109)
XLA Ops:
  6.5 0.0 copy-start.2
  6.5 0.0 all-reduce.2.cloned.1.call-start
  6.5 2.0 collective-permute-start
  8.6 0.7 compare_select_fusion
  9.3 3.8 gather_fusion
  13.0 0.7 compare_and_fusion
  13.7 0.8 select_convert_fusion
  14.5 0.0 all-reduce.2.cloned.1.call-update
  14.5 0.0 copy-done.2
  14.5 0.0 copy-start
  14.6 0.5 multiply_reduce_fusion.6
  15.0 3.3 multiply_reduce_fusion.3
  18.4 43.9 %collective-permute-done = bf16[1024,1024]{1,0:T(8,128)(2,1)} collective-permute-done((bf16[1024,1024]{1,0:T(8,128)(2,1)}, bf16[1024,1024]{1,0:T(8,128)(2,1)}, u32[]{:S(2)}, u32[]{:S(2)}) %collective-permute-start) | collective-permute-done | bytes 2097184 | tf_op jit(solution)/shard_map/ppermute | solution.py:12
  62.2 0.0 collective-permute-start.1
  62.2 0.0 copy-done
  62.2 5.0 %multiply_reduce_fusion.2 = f32[2048]{0:T(1024)S(1)} fusion(bf16[2048,1024]{1,0:T(8,128)(2,1)S(1)} %copy-done, bf16[1024,1024]{1,0:T(8,128)(2,1)S(1)} %copy-done.2, f32[1024]{0:T(1024)S(1)} %multiply_reduce_fusion.6, f32[2048]{0:T(1024)S(1)} %multiply_reduce_fusion.3), kind=kOutput, calls=%fused_computation.3 | convolution fusion | flops 4305451008 | bytes 6311936 | tf_op jit(solution)/shard_map/dot_general | solution.py:22
  67.3 279.0 %all-reduce.2.cloned.1.call-done = bf16[128,1024]{1,0:T(8,128)(2,1)} async-done(((bf16[128,1024]{1,0:T(8,128)(2,1)}), bf16[128,1024]{1,0:T(8,128)(2,1)}) %all-reduce.2.cloned.1.call-update) | async-done | bytes 262160 | tf_op jit(solution)/shard_map/psum | solution.py:43
  346.3 0.0 copy-start.1
  346.3 1.2 multiply_reduce_fusion.7
  347.5 3.9 fusion.3
  351.4 2.1 multiply_reduce_fusion.5
  353.5 0.0 copy-done.1
  353.5 6.6 %multiply_reduce_fusion.1 = f32[2048]{0:T(1024)S(1)} fusion(bf16[2048,1024]{1,0:T(8,128)(2,1)S(1)} %copy-done.1, bf16[1024,1024]{1,0:T(8,128)(2,1)} %collective-permute-done, f32[1024]{0:T(1024)S(1)} %multiply_reduce_fusion.5, f32[2048]{0:T(1024)S(1)} %multiply_reduce_fusion.3), kind=kOutput, calls=%fused_computation.2 | convolution fusion | flops 4305451008 | bytes 6311936 | tf_op jit(solution)/shard_map/dot_general | solution.py:22
  360.2 0.0 collective-permute-done.1
  360.2 2.1 multiply_reduce_fusion.4
  362.2 6.6 %multiply_reduce_fusion = f32[2048]{0:T(1024)S(1)} fusion(bf16[2048,1024]{1,0:T(8,128)(2,1)S(1)} %copy-done.1, bf16[1024,1024]{1,0:T(8,128)(2,1)} %collective-permute-done.1, f32[1024]{0:T(1024)S(1)} %multiply_reduce_fusion.4, f32[2048]{0:T(1024)S(1)} %multiply_reduce_fusion.3), kind=kOutput, calls=%fused_computation.1 | convolution fusion | flops 4305451008 | bytes 6311936 | tf_op jit(solution)/shard_map/dot_general | solution.py:22
  368.9 27.1 %pmin.7 = f32[2048]{0:T(1024)} all-reduce(f32[2048]{0:T(1024)S(1)} %minimum_minimum_fusion), channel_id=1, replica_groups=mesh['grp'=4,'blk'=32] {'grp'}, use_global_device_ids=true, to_apply=%region_10.11 | all-reduce | flops 2048 | bytes 16384 | tf_op jit(solution)/shard_map/pmin | solution.py:46
  (2 shorter events, 0.0 us)
Async XLA Ops:
  6.5 8.0 %copy-start.2 = (bf16[1024,1024]{1,0:T(8,128)(2,1)S(1)}, bf16[1024,1024]{1,0:T(8,128)(2,1)}, u32[]{:S(2)}) copy-start(bf16[1024,1024]{1,0:T(8,128)(2,1)} %param.4) | copy-start | bytes 6291460
  6.5 339.7 %all-reduce.2.cloned.1.call-start = ((), (), s32[]{:S(2)}) async-start(), calls=%async_computation | async-start | bytes 524288 | tf_op jit(solution)/shard_map/psum | solution.py:43
  6.5 55.7 %collective-permute-start = (bf16[1024,1024]{1,0:T(8,128)(2,1)}, bf16[1024,1024]{1,0:T(8,128)(2,1)}, u32[]{:S(2)}, u32[]{:S(2)}) collective-permute-start(bf16[1024,1024]{1,0:T(8,128)(2,1)} %param.4), channel_id=1, source_target_pairs={{31,0},{0,1},{1,2},{2,3},{3,4},{4,5},{5,6},{6,7},{7,8},{8,9},{9,10... | collective-permute-start | bytes 6291464 | tf_op jit(solution)/shard_map/ppermute | solution.py:12
  14.5 47.7 %copy-start = (bf16[2048,1024]{1,0:T(8,128)(2,1)S(1)}, bf16[2048,1024]{1,0:T(8,128)(2,1)}, u32[]{:S(2)}) copy-start(bf16[2048,1024]{1,0:T(8,128)(2,1)} %param.3) | copy-start | bytes 12582916
  62.2 297.9 %collective-permute-start.1 = (bf16[1024,1024]{1,0:T(8,128)(2,1)}, bf16[1024,1024]{1,0:T(8,128)(2,1)}, u32[]{:S(2)}, u32[]{:S(2)}) collective-permute-start(bf16[1024,1024]{1,0:T(8,128)(2,1)} %collective-permute-done), channel_id=1, source_target_pairs={{31,0},{0,1},{1,2},{2,3},{3,4},{4,5},{5,6},{6,7},{7,8},{8,9},{9,10... | collective-permute-start | bytes 6291464 | tf_op jit(solution)/shard_map/ppermute | solution.py:12
  346.3 7.2 %copy-start.1 = (bf16[2048,1024]{1,0:T(8,128)(2,1)S(1)}, bf16[2048,1024]{1,0:T(8,128)(2,1)}, u32[]{:S(2)}) copy-start(bf16[2048,1024]{1,0:T(8,128)(2,1)} %param.3) | copy-start | bytes 12582916
Sparse Core Ops, SparseCore 0:
  14.7 331.5 all-reduce.1
where the time goes:
time: 403 us
  waiting for transfers between devices  323 us (80%)
  blocking collectives  27.1 us (7%)
  matrix products  22.2 us (6%)
  between operations  13.5 us (3%)
  other arithmetic  11.3 us (3%)
    psum x1, waiting for transfers between devices, body(): pick_rows = lax.psum(chosen.astype(jnp.bfloat16), 'blk')  279 us
    ppermute x2, waiting for transfers between devices, from_behind(): return lax.ppermute(block, axis, route)  43.9 us
    pmin x1, blocking collectives, body(): combined = lax.pmin(combined, 'grp')  27.1 us
    dot_general x4, matrix products, least(): lax.dot_general(rows, others, (((1,), (1,)), ((), ())), preferred_element...  22.2 us
    reduce_sum x5, other arithmetic, squares(): return jnp.sum(wide * wide, axis=1)  9.17 us
  transfers between devices with their start and end apart: 3, of which 2 were waited for; matrix products, arithmetic and copies ran while one was open for 7% of the time, Pallas kernels for 0%

commit v1 on v0

v1 whole, which is shorter than its diff:
```python
import jax
import jax.numpy as jnp
from jax import lax
from jax.experimental import pallas as pl
from jax.experimental.pallas import tpu as pltpu
from jax.sharding import PartitionSpec as P

MESH = pl.DeviceIdType.MESH
F32 = jnp.float32
BF16 = jnp.bfloat16

D = 1024
HALF = 1024
T1 = 256
T2 = 128
TC = 128
Q = 64
NM = (T1 + TC) // Q
NP = (T2 + TC) // Q
NT1 = T1 // Q
NT2 = T2 // Q
PK = 32
LT = 512
COLS = 256


def minus_off(role, i):
    if i < NT1:
        return role * T1 + i * Q
    return 2 * T1 + 2 * T2 + role * TC + (i - NT1) * Q


def plus_off(role, i):
    if i < NT2:
        return 2 * T1 + role * T2 + i * Q
    return 2 * T1 + 2 * T2 + (1 - role) * TC + (i - NT2) * Q


def kernel(
    u_hbm, l_hbm, picks_ref, out_ref,
    u, lab, hsq, recv, relay, onecol, pc, pr, ps, py, pz, pp, pq, pmat, psq,
    usq, res, inres, comb, incomb,
    loc_sem, lsem, m1s, m1r, m2s, m2r, p1s, p1r, p2s, p2r, p3s, p3r, ys, yr,
    xs, xr, gs, gr, rs, rr, fs, fr,
):
    g = lax.axis_index("grp")
    b = lax.axis_index("blk")
    yl = g // 2
    k = g % 2
    x = b % 4
    line = b // 4
    yh = line % 2
    z = line // 2

    def dev(yl_, b_, k_=None):
        return (yl_ * 2 + (k if k_ is None else k_), b_)

    def flip(c):
        return jnp.where(c, 1 - yl, yl)

    first, last = x == 0, x == 3
    core = dev(yl, b, 1 - k)
    yside = dev(1 - yl, b)
    ydiag = dev(1 - yl, b, 1 - k)
    back = dev(flip(first), (b + 31) % 32)
    ahead = dev(flip(last), (b + 1) % 32)
    back2 = dev(flip(x < 2), (b + 30) % 32)
    ahead2 = dev(flip(x >= 2), (b + 2) % 32)
    xp = [dev(yl, line * 4 + (x + d) % 4) for d in (1, 2, 3)]
    srcx = (x + 3) % 4
    onward = dev(flip(srcx < 2), (line * 4 + srcx + 30) % 32)
    far = (b + 2) % 32
    server = dev(flip(x >= 2), far // 4 * 4 + (far % 4 + 1) % 4)
    hi = dev(1 - yl, (z * 2 + (1 - yh)) * 4 + x)
    zp = [dev(yl, (((z + d) % 4) * 2 + yh) * 4 + x) for d in (1, 2, 3)]
    role1 = jnp.where(last, 1 - yl, yl)
    role2 = jnp.where(x >= 2, 1 - yl, yl)
    roles = (role1, role2)

    def local(src, dst, i):
        return pltpu.make_async_copy(src, dst, loc_sem.at[i])

    def remote(src, dst, s, r, to):
        return pltpu.make_async_remote_copy(
            src_ref=src, dst_ref=dst, send_sem=s, recv_sem=r,
            device_id=to, device_id_type=MESH,
        )

    def rows(ref, off):
        return ref.at[pl.ds(pl.multiple_of(off, Q), Q)]

    load_u = local(u_hbm, u, 0)
    load_l = local(l_hbm, lab.at[0], 1)
    load_u.start()
    load_l.start()

    peers = [core, yside, ydiag, back, ahead, back2, ahead2, onward, server, hi] + xp + zp
    barrier = pltpu.get_barrier_semaphore()
    for to in peers:
        pl.semaphore_signal(barrier, inc=1, device_id=to, device_id_type=MESH)
    pl.semaphore_wait(barrier, len(peers))

    started = []

    def go(copy):
        copy.start()
        started.append(copy)

    def minus1(i):
        off = minus_off(yl, i)
        return remote(rows(u_hbm, k * HALF + off), rows(recv.at[0], off), m1s.at[i], m1r.at[i], back)

    def minus1_in(i):
        ref = rows(recv.at[0], minus_off(role1, i))
        return remote(ref, ref, m1s.at[i], m1r.at[i], back)

    def minus2(i):
        off = minus_off(role1, i)
        return remote(rows(recv.at[0], off), rows(recv.at[1], off), m2s.at[i], m2r.at[i], back)

    def minus2_in(i):
        ref = rows(recv.at[1], minus_off(role2, i))
        return remote(ref, ref, m2s.at[i], m2r.at[i], back)

    def plus1(i):
        off = plus_off(yl, i)
        return remote(rows(u_hbm, k * HALF + off), relay.at[pl.ds(i * Q, Q)], p1s.at[i], p1r.at[i], xp[0])

    def plus2(i):
        off = plus_off(yl, i)
        return remote(relay.at[pl.ds(i * Q, Q)], rows(recv.at[1], off), p2s.at[i], p2r.at[i], onward)

    def plus2_in(i):
        ref = rows(recv.at[1], plus_off(role2, i))
        return remote(ref, ref, p2s.at[i], p2r.at[i], onward)

    def plus3(i):
        off = plus_off(role2, i)
        return remote(rows(recv.at[1], off), rows(recv.at[0], off), p3s.at[i], p3r.at[i], ahead)

    def plus3_in(i):
        ref = rows(recv.at[0], plus_off(role1, i))
        return remote(ref, ref, p3s.at[i], p3r.at[i], ahead)

    def across(s, j):
        role = roles[s]
        off = minus_off(role, j) if j < NT1 else plus_off(role, j - NT1)
        ref = rows(recv.at[s], off)
        return remote(ref, ref, ys.at[s, j], yr.at[s, j], yside)

    def across_in(s, j):
        role = 1 - roles[s]
        off = minus_off(role, j) if j < NT1 else plus_off(role, j - NT1)
        ref = rows(recv.at[s], off)
        return remote(ref, ref, ys.at[s, j], yr.at[s, j], yside)

    def on_m1(i):
        minus1_in(i).wait_recv()
        if i < NT1:
            go(across(0, i))
        go(minus2(i))

    def on_m2(i):
        minus2_in(i).wait_recv()
        if i < NT1:
            go(across(1, i))

    def on_p1(i):
        plus1(i).wait_recv()
        go(plus2(i))

    def on_p2(i):
        plus2_in(i).wait_recv()
        go(plus3(i))
        if i < NT2:
            go(across(1, NT1 + i))

    def on_p3(i):
        plus3_in(i).wait_recv()
        if i < NT2:
            go(across(0, NT1 + i))

    def on_y(s, js):
        for j in js:
            across_in(s, j).wait_recv()

    t1s = range(NT1)
    t2s = range(NT1, NT1 + NT2)

    swap_l = remote(l_hbm, lab.at[1], lsem.at[0], lsem.at[1], core)
    go(swap_l)
    for i in range(max(NM, NP)):
        if i < NM:
            go(minus1(i))
        if i < NP:
            go(plus1(i))

    quarter = (yl + yh) % 2 * 2 + k
    wide = jnp.broadcast_to(picks_ref[...], (128, 128))
    onecol[...] = wide.T
    mine = onecol[pl.ds(pl.multiple_of(quarter * PK, PK), PK), :]
    lane = lax.broadcasted_iota(jnp.int32, (PK, 128), 1)
    n_rows = u.shape[0]
    load_u.wait()
    KT = 512

    for j in range(4):
        def gather(t, acc):
            base = b * n_rows + t * KT
            hot = jnp.concatenate(
                [jnp.where(mine == lane + (base + c * 128), 1.0, 0.0) for c in range(KT // 128)], axis=1
            ).astype(BF16)
            return acc + jnp.dot(
                hot, u[pl.ds(pl.multiple_of(t * KT, KT), KT), j * 256:(j + 1) * 256],
                preferred_element_type=F32,
            )
        pc[j] = lax.fori_loop(0, n_rows // KT, gather, jnp.zeros((PK, 256), F32)).astype(BF16)

    def pick_x(d):
        return remote(pc.at[(x + d) % 4], pr.at[d - 1], xs.at[d - 1], xr.at[d - 1], xp[d - 1])

    def pick_y():
        return remote(ps.at[0], py, xs.at[3], xr.at[3], hi)

    def pick_z(d):
        return remote(ps.at[1], pz.at[d - 1], xs.at[3 + d], xr.at[3 + d], zp[d - 1])

    def pick_g(d):
        return remote(pp.at[x], pp.at[x], gs.at[d - 1], gr.at[d - 1], xp[d - 1])

    def pick_g_in(d):
        ref = pp.at[(x + 4 - d) % 4]
        return remote(ref, ref, gs.at[d - 1], gr.at[d - 1], xp[d - 1])

    def pick_c():
        return remote(pp, pq, gs.at[3], gr.at[3], core)

    for d in (1, 2, 3):
        go(pick_x(d))

    def half_squares(i):
        def step(t, c):
            r = pl.ds(pl.multiple_of(t * 128, 128), 128)
            w = lab[i, r, :].astype(F32)
            s = 0.5 * jnp.sum(w * w, axis=1, keepdims=True)
            hsq[pl.ds(pl.multiple_of(i * HALF + t * 128, 128), 128), :] = jnp.broadcast_to(s, (128, 128))
            return c
        lax.fori_loop(0, HALF // 128, step, 0)

    def task(src, slot, n=COLS):
        def step(t, best):
            h = hsq[pl.ds(pl.multiple_of(t * LT, LT), LT), :]
            i, r = t // (HALF // LT), t % (HALF // LT)
            v = lab[i, pl.ds(pl.multiple_of(r * LT, LT), LT), :]
            inner = lax.dot_general(v, src[...], (((1,), (1,)), ((), ())), preferred_element_type=F32)
            parts = []
            for c in range(n // 128):
                part = h - inner[:, c * 128:(c + 1) * 128]
                parts.append(jnp.min(part.reshape(LT // 8, 8, 128), axis=0))
            return jnp.minimum(best, jnp.concatenate(parts, axis=1))
        best = lax.fori_loop(0, 2 * HALF // LT, step, jnp.full((8, n), jnp.inf, F32))
        best = jnp.min(best, axis=0, keepdims=True)
        s, row = slot
        for c in range(n // 128):
            res[s, pl.ds(row + c, 1), :] = best[:, c * 128:(c + 1) * 128]

    def own(j):
        task(u.at[pl.ds(pl.multiple_of(k * HALF + j * COLS, COLS), COLS)], (2, 2 * j))

    def got_t1(s, role):
        task(recv.at[s, pl.ds(pl.multiple_of(role * T1, T1), T1)], (s, 2 * role))

    def got_t2(s):
        task(recv.at[s, pl.ds(2 * T1, COLS)], (s, 4))

    def got_c(s):
        task(recv.at[s, pl.ds(2 * T1 + 2 * T2, COLS)], (s, 6))

    def result(s):
        to = (ahead, ahead2)[s]
        return remote(res.at[s], inres.at[s], rs.at[s], rr.at[s], to)

    load_l.wait()
    half_squares(0)
    on_m1(0)
    on_p1(0)

    def own_squares(i, c):
        w = u[pl.ds(pl.multiple_of(k * HALF + i * 128, 128), 128), :].astype(F32)
        w = w * w
        s = w[:, 0:128]
        for c_ in range(1, D // 128):
            s = s + w[:, c_ * 128:(c_ + 1) * 128]
        usq[pl.ds(i, 1), :] = jnp.sum(s.T, axis=0, keepdims=True)
        return c
    lax.fori_loop(0, HALF // 128, own_squares, 0)
    swap_l.wait_recv()
    half_squares(1)
    on_m1(1)
    on_p1(1)
    for d in (1, 2, 3):
        pick_x(d).wait_recv()
    ps[0] = pc[x] + pr[0] + pr[1] + pr[2]
    go(pick_y())
    own(0)
    own(1)
    on_m1(2)
    on_p1(2)
    pick_y().wait_recv()
    ps[1] = ps[0] + py[...]
    for d in (1, 2, 3):
        go(pick_z(d))
    own(2)
    on_m1(3)
    on_p1(3)
    for d in (1, 2, 3):
        pick_z(d).wait_recv()
    pp[x] = ps[1] + pz[0] + pz[1] + pz[2]
    for d in (1, 2, 3):
        go(pick_g(d))
    own(3)
    on_m1(4)
    on_p2(0)
    got_t1(0, role1)
    on_m1(5)
    on_p2(1)
    for d in (1, 2, 3):
        pick_g_in(d).wait_recv()
    go(pick_c())
    on_y(0, t1s)
    got_t1(0, 1 - role1)
    on_m2(0)
    on_p2(2)
    on_y(1, t2s)
    got_t2(1)
    on_m2(1)
    on_p2(3)

    pick_c().wait_recv()
    for j in range(4):
        pmat[0:PK, j * 256:(j + 1) * 256] = pp[j]
        pmat[PK:2 * PK, j * 256:(j + 1) * 256] = pq[j]
    w = pmat[...].astype(F32)
    psq[...] = jnp.broadcast_to(0.5 * jnp.sum(w * w, axis=1, keepdims=True), (2 * PK, 128))

    def pick_task(j, c):
        v = u[pl.ds(pl.multiple_of(k * HALF + j * COLS, COLS), COLS), :]
        inner = lax.dot_general(pmat[...], v, (((1,), (1,)), ((), ())), preferred_element_type=F32)
        for c_ in range(COLS // 128):
            part = jnp.min(psq[...] - inner[:, c_ * 128:(c_ + 1) * 128], axis=0, keepdims=True)
            at = pl.ds(2 * j + c_, 1)
            res[2, at, :] = jnp.minimum(res[2, at, :], part)
        return c
    lax.fori_loop(0, HALF // COLS, pick_task, 0)

    on_m2(2)
    on_p3(0)
    on_m2(3)
    on_p3(1)
    got_t1(1, role2)
    on_m2(4)
    on_p3(2)
    on_y(1, t1s)
    got_t1(1, 1 - role2)
    on_m2(5)
    on_p3(3)
    got_c(1)
    go(result(1))
    got_c(0)
    on_y(0, t2s)
    got_t2(0)
    go(result(0))

    result(1).wait_recv()
    result(0).wait_recv()
    least = jnp.minimum(jnp.minimum(inres[0], inres[1]), res[2])
    comb[...] = (usq[...] + 2.0 * least) * (1.0 / D)
    finals = [
        remote(comb, incomb.at[i], fs.at[i], fr.at[i], to)
        for i, to in enumerate((core, yside, ydiag))
    ]
    for copy in finals:
        go(copy)
    for copy in finals:
        copy.wait_recv()
    out_ref[k] = jnp.minimum(comb[...], incomb[1])
    out_ref[1 - k] = jnp.minimum(incomb[0], incomb[2])
    for copy in started:
        copy.wait_send()


def body(unlabeled, labeled, picks):
    n_rows = unlabeled.shape[0]
    dma = pltpu.SemaphoreType.DMA
    vm = pltpu.VMEM
    out = pl.pallas_call(
        kernel,
        out_shape=jax.ShapeDtypeStruct((2, 8, 128), F32),
        in_specs=[
            pl.BlockSpec(memory_space=pl.ANY),
            pl.BlockSpec(memory_space=pl.ANY),
            pl.BlockSpec(memory_space=pltpu.VMEM),
        ],
        out_specs=pl.BlockSpec(memory_space=pltpu.VMEM),
        scratch_shapes=[
            vm((n_rows, D), BF16), vm((2, HALF, D), BF16), vm((2 * HALF, 128), F32),
            vm((2, HALF, D), BF16), vm((NP * Q, D), BF16), vm((128, 128), jnp.int32),
            vm((4, PK, 256), BF16), vm((3, PK, 256), BF16), vm((2, PK, 256), BF16),
            vm((PK, 256), BF16), vm((3, PK, 256), BF16), vm((4, PK, 256), BF16),
            vm((4, PK, 256), BF16), vm((2 * PK, D), BF16), vm((2 * PK, 128), F32),
            vm((8, 128), F32), vm((3, 8, 128), F32), vm((2, 8, 128), F32),
            vm((8, 128), F32), vm((3, 8, 128), F32),
            dma((2,)), dma((2,)), dma((NM,)), dma((NM,)), dma((NM,)), dma((NM,)),
            dma((NP,)), dma((NP,)), dma((NP,)), dma((NP,)), dma((NP,)), dma((NP,)),
            dma((2, NT1 + NT2)), dma((2, NT1 + NT2)),
            dma((7,)), dma((7,)), dma((4,)), dma((4,)), dma((2,)), dma((2,)), dma((3,)), dma((3,)),
        ],
        compiler_params=pltpu.CompilerParams(
            collective_id=0, has_side_effects=True, vmem_limit_bytes=48 << 20
        ),
    )(unlabeled, labeled, picks.reshape(1, -1))
    return out.reshape(-1)


def solution(mesh):
    return jax.shard_map(
        body,
        mesh=mesh,
        in_specs=(P("blk", None), P(("grp", "blk"), None), P()),
        out_specs=P("blk"),
        check_vma=False,
    )
```

time: 403 us -> 105 us (0.26)
  waiting for transfers between devices: 323 us -> 0 us
  Pallas kernels: 0 us -> 102 us
  blocking collectives: 27.1 us -> 0 us
  matrix products: 22.2 us -> 0 us
  between operations: 13.5 us -> 0.01 us
  other arithmetic: 11.3 us -> 0 us
    psum x1 -> x0, waiting for transfers between devices: 279 us -> none  [body(): pick_rows = lax.psum(chosen.astype(jnp.bfloat16), 'blk')]
    pallas_call x0 -> x1, Pallas kernels: none -> 102 us  [body(): pl.pallas_call(kernel, out_shape=jax.ShapeDtypeStruct((2, 8, 128), F32),...]
    ppermute x2 -> x0, waiting for transfers between devices: 43.9 us -> none  [from_behind(): return lax.ppermute(block, axis, route)]
    pmin x1 -> x0, blocking collectives: 27.1 us -> none  [body(): combined = lax.pmin(combined, 'grp')]
    dot_general x4 -> x0, matrix products: 22.2 us -> none  [least(): lax.dot_general(rows, others, (((1,), (1,)), ((), ())), preferred_element...]
    reduce_sum x5 -> x0, other arithmetic: 9.17 us -> none  [squares(): return jnp.sum(wide * wide, axis=1)]
  transfers between devices with their start and end apart: 3 -> 0, of which waited for: 2 -> 0; matrix products, arithmetic and copies ran while one was open for 7% -> 0% of each run, Pallas kernels for 0% -> 0%
where the time goes in v1:
time: 105 us
  Pallas kernels  102 us (97%)
  local copies, waits for them, and re-layouts  2.85 us (3%)
    pallas_call x1, Pallas kernels, body(): pl.pallas_call(kernel, out_shape=jax.ShapeDtypeStruct((2, 8, 128), F32),...  102 us
    unnamed x5, local copies, waits for them, and re-layouts  2.85 us

profile of v1, /device:TPU:1, one launch (start us, length us, event | category | flops | bytes accessed | tf_op | source)
XLA Modules:
  0.0 104.5 jit_solution(15145313367516329383)
XLA Ops:
  0.0 0.0 copy-start
  0.0 1.6 %copy-done = bf16[1024,1024]{1,0:T(8,128)(2,1)S(1)} copy-done((bf16[1024,1024]{1,0:T(8,128)(2,1)S(1)}, bf16[1024,1024]{1,0:T(8,128)(2,1)}, u32[]{:S(2)}) %copy-start) | copy-done | bytes 2097176
  1.6 0.0 copy-start.1
  1.6 0.7 copy-done.1
  2.2 101.6 %shard_map.37 = f32[2,8,128]{2,1,0:T(8,128)S(1)} custom-call(bf16[2048,1024]{1,0:T(8,128)(2,1)} %u_hbm.1, bf16[1024,1024]{1,0:T(8,128)(2,1)S(1)} %copy-done, s32[1,128]{1,0:T(1,128)S(1)} %bitcast.3), custom_call_target="tpu_custom_call" | custom-call | tf_op jit(solution)/shard_map/pallas_call | solution.py:396
  103.9 0.6 copy.5
Async XLA Ops:
  0.0 1.6 %copy-start = (bf16[1024,1024]{1,0:T(8,128)(2,1)S(1)}, bf16[1024,1024]{1,0:T(8,128)(2,1)}, u32[]{:S(2)}) copy-start(bf16[1024,1024]{1,0:T(8,128)(2,1)} %l_hbm.1) | copy-start | bytes 6291460
  1.6 0.7 copy-start.1

commit v2 on v1

--- a/solution.py
+++ b/solution.py
@@ -14,7 +14,8 @@
 T1 = 256
 T2 = 128
 TC = 128
-Q = 64
+Q = 32
+AHEAD = 3
 NM = (T1 + TC) // Q
 NP = (T2 + TC) // Q
 NT1 = T1 // Q
@@ -22,6 +23,20 @@
 PK = 32
 LT = 512
 COLS = 256
+
+ORDER = (
+    ("gather",), ("hsq0",), ("usq",), ("m1", 0), ("p1", 0), ("m1", 1), ("p1", 1), ("L", 0), ("hsq1",),
+    ("y0", 0), ("m1", 2), ("p1", 2), ("own0",), ("y0", 1), ("m1", 3), ("p1", 3), ("own1",), ("y0", 2),
+    ("m2", 0), ("p2", 0), ("own2",), ("m1", 4), ("p1", 4), ("y0", 3), ("m2", 1), ("p2", 1), ("own3",),
+    ("y1", 0), ("m1", 5), ("p1", 5), ("y1", 8), ("m2", 2), ("p2", 2), ("y0", 4), ("m1", 6), ("p1", 6),
+    ("y1", 1), ("m2", 3), ("p2", 3), ("px", 0), ("y1", 9), ("p3", 0), ("m1", 7), ("A0",), ("y0", 5),
+    ("m2", 4), ("p1", 7), ("y1", 2), ("p2", 4), ("m1", 8), ("y1", 10), ("p3", 1), ("m2", 5), ("y0", 6),
+    ("p2", 5), ("m1", 9), ("py", 0), ("y1", 3), ("p3", 2), ("m2", 6), ("y1", 11), ("E1",), ("p2", 6),
+    ("m1", 10), ("y0", 8), ("p3", 3), ("m2", 7), ("A1",), ("y0", 7), ("p2", 7), ("m1", 11), ("y1", 4),
+    ("B0",), ("p3", 4), ("m2", 8), ("y0", 9), ("p3", 5), ("m2", 9), ("pz", 0), ("y1", 5), ("p3", 6),
+    ("m2", 10), ("y0", 10), ("p3", 7), ("m2", 11), ("F1",), ("y1", 6), ("F0",), ("y0", 11), ("y1", 7),
+    ("B1",), ("E0",), ("pg", 0), ("pc", 0), ("psq",), ("ptask",),
+)
 
 
 def minus_off(role, i):
@@ -67,10 +82,10 @@
     back2 = dev(flip(x < 2), (b + 30) % 32)
     ahead2 = dev(flip(x >= 2), (b + 2) % 32)
     xp = [dev(yl, line * 4 + (x + d) % 4) for d in (1, 2, 3)]
-    srcx = (x + 3) % 4
-    onward = dev(flip(srcx < 2), (line * 4 + srcx + 30) % 32)
-    far = (b + 2) % 32
-    server = dev(flip(x >= 2), far // 4 * 4 + (far % 4 + 1) % 4)
+    relay_to = dev(flip(x < 2), jnp.where(x < 2, (b + 29) % 32, line * 4 + (x + 1) % 4))
+    fed = (x == 1) | (x == 2)
+    relay_from = dev(flip(fed), jnp.where(fed, (b + 3) % 32, line * 4 + (x + 3) % 4))
+    relay_role = flip(fed)
     hi = dev(1 - yl, (z * 2 + (1 - yh)) * 4 + x)
     zp = [dev(yl, (((z + d) % 4) * 2 + yh) * 4 + x) for d in (1, 2, 3)]
     role1 = jnp.where(last, 1 - yl, yl)
@@ -94,7 +109,7 @@
     load_u.start()
     load_l.start()
 
-    peers = [core, yside, ydiag, back, ahead, back2, ahead2, onward, server, hi] + xp + zp
+    peers = [core, yside, ydiag, back, ahead, back2, ahead2, relay_to, relay_from, hi] + xp + zp
     barrier = pltpu.get_barrier_semaphore()
     for to in peers:
         pl.semaphore_signal(barrier, inc=1, device_id=to, device_id_type=MESH)
@@ -124,15 +139,15 @@
 
     def plus1(i):
         off = plus_off(yl, i)
-        return remote(rows(u_hbm, k * HALF + off), relay.at[pl.ds(i * Q, Q)], p1s.at[i], p1r.at[i], xp[0])
+        return remote(rows(u_hbm, k * HALF + off), relay.at[pl.ds(i * Q, Q)], p1s.at[i], p1r.at[i], relay_to)
 
     def plus2(i):
-        off = plus_off(yl, i)
-        return remote(relay.at[pl.ds(i * Q, Q)], rows(recv.at[1], off), p2s.at[i], p2r.at[i], onward)
+        off = plus_off(relay_role, i)
+        return remote(relay.at[pl.ds(i * Q, Q)], rows(recv.at[1], off), p2s.at[i], p2r.at[i], xp[0])
 
     def plus2_in(i):
         ref = rows(recv.at[1], plus_off(role2, i))
-        return remote(ref, ref, p2s.at[i], p2r.at[i], onward)
+        return remote(ref, ref, p2s.at[i], p2r.at[i], xp[0])
 
     def plus3(i):
         off = plus_off(role2, i)
@@ -158,6 +173,8 @@
         minus1_in(i).wait_recv()
         if i < NT1:
             go(across(0, i))
+        if i + AHEAD < NM:
+            go(minus1(i + AHEAD))
         go(minus2(i))
 
     def on_m2(i):
@@ -167,6 +184,8 @@
 
     def on_p1(i):
         plus1(i).wait_recv()
+        if i + AHEAD < NP:
+            go(plus1(i + AHEAD))
         go(plus2(i))
 
     def on_p2(i):
@@ -180,16 +199,9 @@
         if i < NT2:
             go(across(0, NT1 + i))
 
-    def on_y(s, js):
-        for j in js:
-            across_in(s, j).wait_recv()
-
-    t1s = range(NT1)
-    t2s = range(NT1, NT1 + NT2)
-
     swap_l = remote(l_hbm, lab.at[1], lsem.at[0], lsem.at[1], core)
     go(swap_l)
-    for i in range(max(NM, NP)):
+    for i in range(min(AHEAD, NM)):
         if i < NM:
             go(minus1(i))
         if i < NP:
@@ -201,20 +213,21 @@
     mine = onecol[pl.ds(pl.multiple_of(quarter * PK, PK), PK), :]
     lane = lax.broadcasted_iota(jnp.int32, (PK, 128), 1)
     n_rows = u.shape[0]
-    load_u.wait()
     KT = 512
 
-    for j in range(4):
-        def gather(t, acc):
+    def gather_picks():
+        load_u.wait()
+        acc = jnp.zeros((PK, D), F32)
+        for t in range(n_rows // KT):
             base = b * n_rows + t * KT
             hot = jnp.concatenate(
                 [jnp.where(mine == lane + (base + c * 128), 1.0, 0.0) for c in range(KT // 128)], axis=1
             ).astype(BF16)
-            return acc + jnp.dot(
-                hot, u[pl.ds(pl.multiple_of(t * KT, KT), KT), j * 256:(j + 1) * 256],
-                preferred_element_type=F32,
-            )
-        pc[j] = lax.fori_loop(0, n_rows // KT, gather, jnp.zeros((PK, 256), F32)).astype(BF16)
+            acc = acc + jnp.dot(hot, u[t * KT:(t + 1) * KT, :], preferred_element_type=F32)
+        for j in range(4):
+            pc[j] = acc[:, j * 256:(j + 1) * 256].astype(BF16)
+        for d in (1, 2, 3):
+            go(pick_x(d))
 
     def pick_x(d):
         return remote(pc.at[(x + d) % 4], pr.at[d - 1], xs.at[d - 1], xr.at[d - 1], xp[d - 1])
@@ -234,9 +247,6 @@
 
     def pick_c():
         return remote(pp, pq, gs.at[3], gr.at[3], core)
-
-    for d in (1, 2, 3):
-        go(pick_x(d))
 
     def half_squares(i):
         def step(t, c):
@@ -248,17 +258,17 @@
         lax.fori_loop(0, HALF // 128, step, 0)
 
     def task(src, slot, n=COLS):
-        def step(t, best):
-            h = hsq[pl.ds(pl.multiple_of(t * LT, LT), LT), :]
+        best = jnp.full((8, n), jnp.inf, F32)
+        for t in range(2 * HALF // LT):
+            h = hsq[t * LT:(t + 1) * LT, :]
             i, r = t // (HALF // LT), t % (HALF // LT)
-            v = lab[i, pl.ds(pl.multiple_of(r * LT, LT), LT), :]
+            v = lab[i, r * LT:(r + 1) * LT, :]
             inner = lax.dot_general(v, src[...], (((1,), (1,)), ((), ())), preferred_element_type=F32)
             parts = []
             for c in range(n // 128):
                 part = h - inner[:, c * 128:(c + 1) * 128]
                 parts.append(jnp.min(part.reshape(LT // 8, 8, 128), axis=0))
-            return jnp.minimum(best, jnp.concatenate(parts, axis=1))
-        best = lax.fori_loop(0, 2 * HALF // LT, step, jnp.full((8, n), jnp.inf, F32))
+            best = jnp.minimum(best, jnp.concatenate(parts, axis=1))
         best = jnp.min(best, axis=0, keepdims=True)
         s, row = slot
         for c in range(n // 128):
@@ -280,96 +290,86 @@
         to = (ahead, ahead2)[s]
         return remote(res.at[s], inres.at[s], rs.at[s], rr.at[s], to)
 
-    load_l.wait()
-    half_squares(0)
-    on_m1(0)
-    on_p1(0)
-
-    def own_squares(i, c):
-        w = u[pl.ds(pl.multiple_of(k * HALF + i * 128, 128), 128), :].astype(F32)
-        w = w * w
-        s = w[:, 0:128]
-        for c_ in range(1, D // 128):
-            s = s + w[:, c_ * 128:(c_ + 1) * 128]
-        usq[pl.ds(i, 1), :] = jnp.sum(s.T, axis=0, keepdims=True)
-        return c
-    lax.fori_loop(0, HALF // 128, own_squares, 0)
-    swap_l.wait_recv()
-    half_squares(1)
-    on_m1(1)
-    on_p1(1)
-    for d in (1, 2, 3):
-        pick_x(d).wait_recv()
-    ps[0] = pc[x] + pr[0] + pr[1] + pr[2]
-    go(pick_y())
-    own(0)
-    own(1)
-    on_m1(2)
-    on_p1(2)
-    pick_y().wait_recv()
-    ps[1] = ps[0] + py[...]
-    for d in (1, 2, 3):
-        go(pick_z(d))
-    own(2)
-    on_m1(3)
-    on_p1(3)
-    for d in (1, 2, 3):
-        pick_z(d).wait_recv()
-    pp[x] = ps[1] + pz[0] + pz[1] + pz[2]
-    for d in (1, 2, 3):
-        go(pick_g(d))
-    own(3)
-    on_m1(4)
-    on_p2(0)
-    got_t1(0, role1)
-    on_m1(5)
-    on_p2(1)
-    for d in (1, 2, 3):
-        pick_g_in(d).wait_recv()
-    go(pick_c())
-    on_y(0, t1s)
-    got_t1(0, 1 - role1)
-    on_m2(0)
-    on_p2(2)
-    on_y(1, t2s)
-    got_t2(1)
-    on_m2(1)
-    on_p2(3)
-
-    pick_c().wait_recv()
-    for j in range(4):
-        pmat[0:PK, j * 256:(j + 1) * 256] = pp[j]
-        pmat[PK:2 * PK, j * 256:(j + 1) * 256] = pq[j]
-    w = pmat[...].astype(F32)
-    psq[...] = jnp.broadcast_to(0.5 * jnp.sum(w * w, axis=1, keepdims=True), (2 * PK, 128))
-
-    def pick_task(j, c):
-        v = u[pl.ds(pl.multiple_of(k * HALF + j * COLS, COLS), COLS), :]
-        inner = lax.dot_general(pmat[...], v, (((1,), (1,)), ((), ())), preferred_element_type=F32)
-        for c_ in range(COLS // 128):
-            part = jnp.min(psq[...] - inner[:, c_ * 128:(c_ + 1) * 128], axis=0, keepdims=True)
-            at = pl.ds(2 * j + c_, 1)
-            res[2, at, :] = jnp.minimum(res[2, at, :], part)
-        return c
-    lax.fori_loop(0, HALF // COLS, pick_task, 0)
-
-    on_m2(2)
-    on_p3(0)
-    on_m2(3)
-    on_p3(1)
-    got_t1(1, role2)
-    on_m2(4)
-    on_p3(2)
-    on_y(1, t1s)
-    got_t1(1, 1 - role2)
-    on_m2(5)
-    on_p3(3)
-    got_c(1)
-    go(result(1))
-    got_c(0)
-    on_y(0, t2s)
-    got_t2(0)
-    go(result(0))
+    def own_squares():
+        def step(i, c):
+            w = u[pl.ds(pl.multiple_of(k * HALF + i * 128, 128), 128), :].astype(F32)
+            w = w * w
+            t = w[:, 0:128]
+            for c_ in range(1, D // 128):
+                t = t + w[:, c_ * 128:(c_ + 1) * 128]
+            usq[pl.ds(i, 1), :] = jnp.sum(t.T, axis=0, keepdims=True)
+            return c
+        lax.fori_loop(0, HALF // 128, step, 0)
+
+    def first_half_squares():
+        load_l.wait()
+        half_squares(0)
+
+    def on_px(i):
+        for d in (1, 2, 3):
+            pick_x(d).wait_recv()
+        ps[0] = pc[x] + pr[0] + pr[1] + pr[2]
+        go(pick_y())
+
+    def on_py(i):
+        pick_y().wait_recv()
+        ps[1] = ps[0] + py[...]
+        for d in (1, 2, 3):
+            go(pick_z(d))
+
+    def on_pz(i):
+        for d in (1, 2, 3):
+            pick_z(d).wait_recv()
+        pp[x] = ps[1] + pz[0] + pz[1] + pz[2]
+        for d in (1, 2, 3):
+            go(pick_g(d))
+
+    def on_pg(i):
+        for d in (1, 2, 3):
+            pick_g_in(d).wait_recv()
+        go(pick_c())
+
+    def pick_squares():
+        for j in range(4):
+            pmat[0:PK, j * 256:(j + 1) * 256] = pp[j]
+            pmat[PK:2 * PK, j * 256:(j + 1) * 256] = pq[j]
+        w = pmat[...].astype(F32)
+        psq[...] = jnp.broadcast_to(0.5 * jnp.sum(w * w, axis=1, keepdims=True), (2 * PK, 128))
+
+    def pick_tasks():
+        for j in range(HALF // COLS):
+            v = u[pl.ds(pl.multiple_of(k * HALF + j * COLS, COLS), COLS), :]
+            inner = lax.dot_general(pmat[...], v, (((1,), (1,)), ((), ())), preferred_element_type=F32)
+            for c in range(COLS // 128):
+                part = jnp.min(psq[...] - inner[:, c * 128:(c + 1) * 128], axis=0, keepdims=True)
+                row = 2 * j + c
+                res[2, row:row + 1, :] = jnp.minimum(res[2, row:row + 1, :], part)
+
+    events = {
+        "m1": on_m1, "m2": on_m2, "p1": on_p1, "p2": on_p2, "p3": on_p3,
+        "y0": lambda i: across_in(0, i).wait_recv(), "y1": lambda i: across_in(1, i).wait_recv(),
+        "L": lambda i: swap_l.wait_recv(),
+        "px": on_px, "py": on_py, "pz": on_pz, "pg": on_pg, "pc": lambda i: pick_c().wait_recv(),
+    }
+    work = {
+        "gather": gather_picks, "hsq0": first_half_squares, "hsq1": lambda: half_squares(1),
+        "usq": own_squares, "psq": pick_squares, "ptask": pick_tasks,
+        "own0": lambda: own(0), "own1": lambda: own(1), "own2": lambda: own(2), "own3": lambda: own(3),
+        "A0": lambda: got_t1(0, role1), "A1": lambda: got_t1(1, role2),
+        "B0": lambda: got_t1(0, 1 - role1), "B1": lambda: got_t1(1, 1 - role2),
+        "E0": lambda: got_t2(0), "E1": lambda: got_t2(1), "F0": lambda: got_c(0), "F1": lambda: got_c(1),
+    }
+    finished = [0, 0]
+    for step in ORDER:
+        if len(step) == 2:
+            events[step[0]](step[1])
+        else:
+            work[step[0]]()
+            if step[0][0] in "ABEF":
+                s = int(step[0][1])
+                finished[s] += 1
+                if finished[s] == 4:
+                    go(result(s))
 
     result(1).wait_recv()
     result(0).wait_recv()
@@ -416,7 +416,7 @@
             dma((7,)), dma((7,)), dma((4,)), dma((4,)), dma((2,)), dma((2,)), dma((3,)), dma((3,)),
         ],
         compiler_params=pltpu.CompilerParams(
-            collective_id=0, has_side_effects=True, vmem_limit_bytes=48 << 20
+            collective_id=0, has_side_effects=True, vmem_limit_bytes=60 << 20
         ),
     )(unlabeled, labeled, picks.reshape(1, -1))
     return out.reshape(-1)

time: 105 us -> 67.8 us (0.65)
  Pallas kernels: 102 us -> 66.2 us
  local copies, waits for them, and re-layouts: 2.85 us -> 1.3 us
    pallas_call x1, Pallas kernels: 102 us -> 66.2 us  [body(): pl.pallas_call(kernel, out_shape=jax.ShapeDtypeStruct((2, 8, 128), F32),...]
    unnamed x5 -> x1, local copies, waits for them, and re-layouts: 2.85 us -> 1.3 us
where the time goes in v2:
time: 67.8 us; the launch traced here: 67.5 us
  Pallas kernels  66.2 us (98%)
  local copies, waits for them, and re-layouts  1.3 us (2%)
    pallas_call x1, Pallas kernels, body(): pl.pallas_call(kernel, out_shape=jax.ShapeDtypeStruct((2, 8, 128), F32),...  66.2 us

profile of v2, /device:TPU:1, one launch (start us, length us, event | category | flops | bytes accessed | tf_op | source)
XLA Modules:
  0.0 67.5 jit_solution(5923967850728454583)
XLA Ops:
  0.0 66.2 %shard_map.37 = f32[2,8,128]{2,1,0:T(8,128)} custom-call(bf16[2048,1024]{1,0:T(8,128)(2,1)} %u_hbm.1, bf16[1024,1024]{1,0:T(8,128)(2,1)} %l_hbm.1, s32[1,128]{1,0:T(1,128)} %bitcast.3), custom_call_target="tpu_custom_call" | custom-call | tf_op jit(solution)/shard_map/pallas_call | solution.py:396
  66.2 1.3 %copy.5 = f32[2048]{0:T(1024)} copy(f32[2048]{0:T(1024)} %bitcast.2) | data formatting | bytes 16384

commit v3 on v2

--- a/solution.py
+++ b/solution.py
@@ -16,6 +16,7 @@
 TC = 128
 Q = 32
 AHEAD = 3
+LAST = 5
 NM = (T1 + TC) // Q
 NP = (T2 + TC) // Q
 NT1 = T1 // Q
@@ -29,13 +30,13 @@
     ("y0", 0), ("m1", 2), ("p1", 2), ("own0",), ("y0", 1), ("m1", 3), ("p1", 3), ("own1",), ("y0", 2),
     ("m2", 0), ("p2", 0), ("own2",), ("m1", 4), ("p1", 4), ("y0", 3), ("m2", 1), ("p2", 1), ("own3",),
     ("y1", 0), ("m1", 5), ("p1", 5), ("y1", 8), ("m2", 2), ("p2", 2), ("y0", 4), ("m1", 6), ("p1", 6),
-    ("y1", 1), ("m2", 3), ("p2", 3), ("px", 0), ("y1", 9), ("p3", 0), ("m1", 7), ("A0",), ("y0", 5),
-    ("m2", 4), ("p1", 7), ("y1", 2), ("p2", 4), ("m1", 8), ("y1", 10), ("p3", 1), ("m2", 5), ("y0", 6),
-    ("p2", 5), ("m1", 9), ("py", 0), ("y1", 3), ("p3", 2), ("m2", 6), ("y1", 11), ("E1",), ("p2", 6),
-    ("m1", 10), ("y0", 8), ("p3", 3), ("m2", 7), ("A1",), ("y0", 7), ("p2", 7), ("m1", 11), ("y1", 4),
-    ("B0",), ("p3", 4), ("m2", 8), ("y0", 9), ("p3", 5), ("m2", 9), ("pz", 0), ("y1", 5), ("p3", 6),
-    ("m2", 10), ("y0", 10), ("p3", 7), ("m2", 11), ("F1",), ("y1", 6), ("F0",), ("y0", 11), ("y1", 7),
-    ("B1",), ("E0",), ("pg", 0), ("pc", 0), ("psq",), ("ptask",),
+    ("y1", 1), ("m2", 3), ("p2", 3), ("y1", 9), ("p3", 0), ("m1", 7), ("A0",), ("y0", 5), ("m2", 4),
+    ("p1", 7), ("y1", 2), ("p2", 4), ("m1", 8), ("y1", 10), ("p3", 1), ("m2", 5), ("px", 0), ("y0", 6),
+    ("p2", 5), ("m1", 9), ("y1", 11), ("E1",), ("p3", 2), ("m2", 6), ("y0", 8), ("p2", 6), ("m1", 10),
+    ("y0", 7), ("B0",), ("p3", 3), ("m2", 7), ("y0", 9), ("p2", 7), ("m1", 11), ("py", 0), ("A1",),
+    ("y0", 10), ("p3", 4), ("m2", 8), ("y0", 11), ("E0",), ("p3", 5), ("m2", 9), ("y1", 3), ("p3", 6),
+    ("m2", 10), ("y1", 4), ("p3", 7), ("m2", 11), ("F1",), ("y1", 5), ("pz", 0), ("F0",), ("y1", 6),
+    ("y1", 7), ("B1",), ("pg", 0), ("pc", 0), ("psq",), ("ptask",),
 )
 
 
@@ -54,7 +55,7 @@
 def kernel(
     u_hbm, l_hbm, picks_ref, out_ref,
     u, lab, hsq, recv, relay, onecol, pc, pr, ps, py, pz, pp, pq, pmat, psq,
-    usq, res, inres, comb, incomb,
+    res, got, kept, near,
     loc_sem, lsem, m1s, m1r, m2s, m2r, p1s, p1r, p2s, p2r, p3s, p3r, ys, yr,
     xs, xr, gs, gr, rs, rr, fs, fr,
 ):
@@ -79,8 +80,6 @@
     ydiag = dev(1 - yl, b, 1 - k)
     back = dev(flip(first), (b + 31) % 32)
     ahead = dev(flip(last), (b + 1) % 32)
-    back2 = dev(flip(x < 2), (b + 30) % 32)
-    ahead2 = dev(flip(x >= 2), (b + 2) % 32)
     xp = [dev(yl, line * 4 + (x + d) % 4) for d in (1, 2, 3)]
     relay_to = dev(flip(x < 2), jnp.where(x < 2, (b + 29) % 32, line * 4 + (x + 1) % 4))
     fed = (x == 1) | (x == 2)
@@ -109,7 +108,8 @@
     load_u.start()
     load_l.start()
 
-    peers = [core, yside, ydiag, back, ahead, back2, ahead2, relay_to, relay_from, hi] + xp + zp
+    groups = [[(i, (b + d) % 32) for i in range(4)] for d in (1, 2, 30, 31)]
+    peers = [core, yside, ydiag, relay_to, relay_from, hi] + xp + zp + sum(groups, [])
     barrier = pltpu.get_barrier_semaphore()
     for to in peers:
         pl.semaphore_signal(barrier, inc=1, device_id=to, device_id_type=MESH)
@@ -168,6 +168,8 @@
         off = minus_off(role, j) if j < NT1 else plus_off(role, j - NT1)
         ref = rows(recv.at[s], off)
         return remote(ref, ref, ys.at[s, j], yr.at[s, j], yside)
+
+    held, flushed = [], []
 
     def on_m1(i):
         minus1_in(i).wait_recv()
@@ -180,7 +182,10 @@
     def on_m2(i):
         minus2_in(i).wait_recv()
         if i < NT1:
-            go(across(1, i))
+            if i >= NT1 - LAST and not flushed:
+                held.append(i)
+            else:
+                go(across(1, i))
 
     def on_p1(i):
         plus1(i).wait_recv()
@@ -198,6 +203,10 @@
         plus3_in(i).wait_recv()
         if i < NT2:
             go(across(0, NT1 + i))
+        if i == NT2 - 1:
+            flushed.append(i)
+            for j in held:
+                go(across(1, j))
 
     swap_l = remote(l_hbm, lab.at[1], lsem.at[0], lsem.at[1], core)
     go(swap_l)
@@ -287,8 +296,17 @@
         task(recv.at[s, pl.ds(2 * T1 + 2 * T2, COLS)], (s, 6))
 
     def result(s):
-        to = (ahead, ahead2)[s]
-        return remote(res.at[s], inres.at[s], rs.at[s], rr.at[s], to)
+        return [
+            remote(res.at[s], got.at[s, yl, k], rs.at[s, i], rr.at[s, g], to)
+            for i, to in enumerate(groups[s])
+        ]
+
+    def result_in(s, i):
+        ref = got.at[s, i // 2, i % 2]
+        return remote(ref, ref, rs.at[s, i], rr.at[s, i], groups[s][i])
+
+    def share(i, to):
+        return remote(kept, near.at[i], fs.at[i], fr.at[i], to)
 
     def own_squares():
         def step(i, c):
@@ -297,7 +315,7 @@
             t = w[:, 0:128]
             for c_ in range(1, D // 128):
                 t = t + w[:, c_ * 128:(c_ + 1) * 128]
-            usq[pl.ds(i, 1), :] = jnp.sum(t.T, axis=0, keepdims=True)
+            kept[1, pl.ds(i, 1), :] = jnp.sum(t.T, axis=0, keepdims=True)
             return c
         lax.fori_loop(0, HALF // 128, step, 0)
 
@@ -365,26 +383,28 @@
             events[step[0]](step[1])
         else:
             work[step[0]]()
+            if step[0] == "ptask":
+                kept[0] = res[2]
+                for i, to in enumerate((core, yside, ydiag)):
+                    go(share(i, to))
             if step[0][0] in "ABEF":
                 s = int(step[0][1])
                 finished[s] += 1
                 if finished[s] == 4:
-                    go(result(s))
-
-    result(1).wait_recv()
-    result(0).wait_recv()
-    least = jnp.minimum(jnp.minimum(inres[0], inres[1]), res[2])
-    comb[...] = (usq[...] + 2.0 * least) * (1.0 / D)
-    finals = [
-        remote(comb, incomb.at[i], fs.at[i], fr.at[i], to)
-        for i, to in enumerate((core, yside, ydiag))
-    ]
-    for copy in finals:
-        go(copy)
-    for copy in finals:
-        copy.wait_recv()
-    out_ref[k] = jnp.minimum(comb[...], incomb[1])
-    out_ref[1 - k] = jnp.minimum(incomb[0], incomb[2])
+                    for copy in result(s):
+                        go(copy)
+
+    for i, to in enumerate((core, yside, ydiag)):
+        share(i, to).wait_recv()
+    here = jnp.minimum(kept[0], near[1, 0])
+    there = jnp.minimum(near[0, 0], near[2, 0])
+    for s in (1, 0):
+        for i in range(4):
+            result_in(s, i).wait_recv()
+        here = jnp.minimum(here, jnp.minimum(got[s, 0, k], got[s, 1, k]))
+        there = jnp.minimum(there, jnp.minimum(got[s, 0, 1 - k], got[s, 1, 1 - k]))
+    out_ref[k] = (kept[1] + 2.0 * here) * (1.0 / D)
+    out_ref[1 - k] = (near[0, 1] + 2.0 * there) * (1.0 / D)
     for copy in started:
         copy.wait_send()
 
@@ -408,12 +428,11 @@
             vm((4, PK, 256), BF16), vm((3, PK, 256), BF16), vm((2, PK, 256), BF16),
             vm((PK, 256), BF16), vm((3, PK, 256), BF16), vm((4, PK, 256), BF16),
             vm((4, PK, 256), BF16), vm((2 * PK, D), BF16), vm((2 * PK, 128), F32),
-            vm((8, 128), F32), vm((3, 8, 128), F32), vm((2, 8, 128), F32),
-            vm((8, 128), F32), vm((3, 8, 128), F32),
+            vm((3, 8, 128), F32), vm((2, 2, 2, 8, 128), F32), vm((2, 8, 128), F32), vm((3, 2, 8, 128), F32),
             dma((2,)), dma((2,)), dma((NM,)), dma((NM,)), dma((NM,)), dma((NM,)),
             dma((NP,)), dma((NP,)), dma((NP,)), dma((NP,)), dma((NP,)), dma((NP,)),
             dma((2, NT1 + NT2)), dma((2, NT1 + NT2)),
-            dma((7,)), dma((7,)), dma((4,)), dma((4,)), dma((2,)), dma((2,)), dma((3,)), dma((3,)),
+            dma((7,)), dma((7,)), dma((4,)), dma((4,)), dma((2, 4)), dma((2, 4)), dma((3,)), dma((3,)),
         ],
         compiler_params=pltpu.CompilerParams(
             collective_id=0, has_side_effects=True, vmem_limit_bytes=60 << 20

time: 67.8 us -> 64.1 us (0.945)
  Pallas kernels: 66.2 us -> 62.6 us
    pallas_call x1, Pallas kernels: 66.2 us -> 62.6 us  [body(): pl.pallas_call(kernel, out_shape=jax.ShapeDtypeStruct((2, 8, 128), F32),...]
where the time goes in v3:
time: 64.1 us; the launch traced here: 63.9 us
  Pallas kernels  62.6 us (98%)
  local copies, waits for them, and re-layouts  1.3 us (2%)
    pallas_call x1, Pallas kernels, body(): pl.pallas_call(kernel, out_shape=jax.ShapeDtypeStruct((2, 8, 128), F32),...  62.6 us
    unnamed x1, local copies, waits for them, and re-layouts  1.3 us

profile of v3, /device:TPU:1, one launch (start us, length us, event | category | flops | bytes accessed | tf_op | source)
XLA Modules:
  0.0 63.9 jit_solution(16622921722321404854)
XLA Ops:
  0.0 62.6 %shard_map.37 = f32[2,8,128]{2,1,0:T(8,128)} custom-call(bf16[2048,1024]{1,0:T(8,128)(2,1)} %u_hbm.1, bf16[1024,1024]{1,0:T(8,128)(2,1)} %l_hbm.1, s32[1,128]{1,0:T(1,128)} %bitcast.3), custom_call_target="tpu_custom_call" | custom-call | tf_op jit(solution)/shard_map/pallas_call | solution.py:416
  62.6 1.3 %copy.5 = f32[2048]{0:T(1024)} copy(f32[2048]{0:T(1024)} %bitcast.2) | data formatting | bytes 16384
